TPU v7x, 256 devices: a whole 4x4x8 slice. The times are simulated.
256 devices in a mesh: stretch: 64 (over x, z_lo, y), head: 4 (over z_hi, core).
Axes of the slice: x: 4, y: 4, z: 8 (z_hi: 2, z_lo: 4; z = z_hi * 4 + z_lo), core: 2. Of those that a mesh axis runs over, the one named last changes fastest.
Arguments:
- queries: bfloat16 [8192, 6144], P('stretch', 'head'), may hold values from -92 to 92
- keys: bfloat16 [8192, 1024], P('stretch', 'head'), may hold values from -11 to 11
- values: bfloat16 [8192, 1024], P('stretch', 'head'), may hold values from -6 to 6
- cache_keys: bfloat16 [4096, 1024], P(('stretch', 'head')), may hold values from -100 to 100
- cache_values: bfloat16 [4096, 1024], P(('stretch', 'head')), may hold values from -6 to 6
- page_owner: int32 [64], replicated, may hold values from 0 to 63, each once
- window: int32 [4], replicated, may hold values from 1 to 2, as said below
Outputs:
- attended: bfloat16 [8192, 6144], P('stretch', 'head')
Inputs may be any that keep to these rules, and one draw needn't show every extreme that they name: `window`: some in-flight stretch attends all 2 cached stretches.
All inputs are finite; a program needn't handle non-finite values.
Results may differ from a plain program's by a relative error of at most 0.006.
Values may be sent and summed in bfloat16 or wider, within the bound.
No kernel may reach another device: no remote copies, remote signals or barrier semaphores. Data moves between devices by JAX's collectives and lax.ppermute only.
A program may use at most 192 MiB of HBM per device.

v0:
```python
import jax
import jax.numpy as jnp
from jax import lax
from jax.sharding import PartitionSpec as P

D_HEAD = 128
STRETCHES = 4
CACHED = 2


neg_fill = -1e30
key_block = 1024


def absorb(carried, query_block, key_piece, value_piece, visible):
    running_max, running_sum, summed_values = carried
    kv_count = running_max.shape[0]
    head_size = query_block.shape[-1]
    keys_split = key_piece.reshape(key_piece.shape[0], kv_count, head_size)
    values_split = value_piece.reshape(value_piece.shape[0], kv_count, head_size)
    raw_scores = jnp.einsum(
        "qkgd,tkd->kgqt", query_block, keys_split, preferred_element_type=jnp.float32
    )
    masked = jnp.where(visible, raw_scores * head_size ** (-0.5), neg_fill)
    newest = jnp.maximum(running_max, jnp.max(masked, axis=-1))
    shifted = jnp.where(newest > 0.5 * neg_fill, newest, 0.0)
    weights = jnp.exp(masked - shifted[..., None])
    factor = jnp.exp(running_max - shifted)
    running_sum = running_sum * factor + jnp.sum(weights, axis=-1)
    update = jnp.einsum(
        "kgqt,tkd->qkgd",
        weights.astype(jnp.bfloat16),
        values_split,
        preferred_element_type=jnp.float32,
    )
    summed_values = summed_values * jnp.transpose(factor, (2, 0, 1))[..., None] + update
    return (newest, running_sum, summed_values)


def absorb_blocks(carried, query_block, key_piece, value_piece, visible):
    total_rows = key_piece.shape[0]
    for offset in range(0, total_rows, key_block):
        width = min(key_block, total_rows - offset)
        carried = absorb(
            carried,
            query_block,
            key_piece[offset : offset + width],
            value_piece[offset : offset + width],
            visible[offset : offset + width],
        )
    return carried


def empty_state(query_rows, kv_count, group_size, head_size):
    return (
        jnp.full((kv_count, group_size, query_rows), neg_fill, jnp.float32),
        jnp.zeros((kv_count, group_size, query_rows), jnp.float32),
        jnp.zeros((query_rows, kv_count, group_size, head_size), jnp.float32),
    )


def finish(carried):
    running_max, running_sum, summed_values = carried
    result = summed_values / jnp.transpose(running_sum, (2, 0, 1))[..., None]
    return result.reshape(result.shape[0], -1).astype(jnp.bfloat16)


def on_device(queries, keys, values, cache_keys, cache_values, page_owner, window):
    row_count = queries.shape[0]
    kv_count = keys.shape[1] // D_HEAD
    group_size = queries.shape[1] // keys.shape[1]
    devices = lax.axis_size("stretch")
    my_index = lax.axis_index("stretch")
    stretch_rows = row_count * devices // STRETCHES
    slot_ids = jnp.arange(devices, dtype=jnp.int32)
    logical = jnp.sum(
        jnp.where(page_owner[None, :] == slot_ids[:, None], slot_ids[None, :], 0), axis=1
    )
    cached_of_slot = logical // (devices // CACHED)
    cache_k, cache_v = (
        lax.all_to_all(cache_keys, "head", split_axis=1, concat_axis=0, tiled=True),
        lax.all_to_all(cache_values, "head", split_axis=1, concat_axis=0, tiled=True),
    )
    page_rows = cache_k.shape[0]
    query_sets = (
        (
            queries.reshape(queries.shape[0], kv_count, group_size, D_HEAD),
            my_index * row_count // stretch_rows,
        ),
    )

    def fresh_visible(piece_rows, stretch_group):
        return jnp.arange(piece_rows, dtype=jnp.int32) // stretch_rows <= stretch_group

    def take_fresh(states, pieces, first_row):
        key_piece, value_piece = pieces
        results = []
        for carried, (query_block, stretch_group) in zip(states, query_sets):
            visible = fresh_visible(key_piece.shape[0], stretch_group)
            carried = lax.cond(
                first_row // stretch_rows > stretch_group,
                lambda carried_in: carried_in,
                lambda carried_in: absorb_blocks(
                    carried_in, query_block, key_piece, value_piece, visible
                ),
                carried,
            )
            results.append(carried)
        return tuple(results)

    states = tuple(
        (
            empty_state(query_block.shape[0], kv_count, group_size, D_HEAD)
            for query_block, stretch_group in query_sets
        )
    )
    key_piece = lax.all_gather(cache_k, "stretch", axis=0, tiled=True)
    value_piece = lax.all_gather(cache_v, "stretch", axis=0, tiled=True)
    results = []
    for take_carried, (query_block, stretch_group) in zip(states, query_sets):
        slot_of_row = jnp.arange(key_piece.shape[0], dtype=jnp.int32) // page_rows
        cached = jnp.sum(
            jnp.where(slot_of_row[:, None] == slot_ids[None, :], cached_of_slot[None, :], 0), axis=1
        )
        visible = cached >= CACHED - window[stretch_group]
        results.append(absorb_blocks(take_carried, query_block, key_piece, value_piece, visible))
    states = take_fresh(
        tuple(results),
        (
            lax.all_gather(keys, "stretch", axis=0, tiled=True),
            lax.all_gather(values, "stretch", axis=0, tiled=True),
        ),
        jnp.int32(0),
    )
    outputs = [finish(carried) for carried in states]
    return outputs[0]


def solution(mesh):
    return jax.shard_map(
        on_device,
        mesh=mesh,
        in_specs=(
            P("stretch", "head"),
            P("stretch", "head"),
            P("stretch", "head"),
            P(("stretch", "head"), None),
            P(("stretch", "head"), None),
            P(),
            P(),
        ),
        out_specs=P("stretch", "head"),
        check_vma=False,
    )
```

profile of v0, /device:TPU:8, one launch (start us, length us, event | category | flops | bytes accessed | tf_op | source)
XLA Modules:
  0.0 1361.1 jit_solution(8657701112437971570)
XLA Ops:
  7.3 16.2 %all_to_all.38 = bf16[16,4,256]{2,0,1:T(8,128)(2,1)} all-to-all(bf16[16,4,256]{2,0,1:T(8,128)(2,1)S(1)} %bitcast.512), channel_id=1, replica_groups=mesh['stretch'=64,'head'=4] {'head'}, dimensions={1} | all-to-all | bytes 65536 | tf_op jit(solution)/shard_map/all_to_all | solution.py:81
  24.3 10.9 all_to_all.39
  35.3 1.6 copy.211
  36.9 1.6 copy.239
  42.8 327.1 %all-gather.7.cloned.1.call-done = bf16[4096,256]{1,0:T(8,128)(2,1)} async-done(((bf16[64,256]{1,0:T(8,128)(2,1)}), bf16[4096,256]{1,0:T(8,128)(2,1)}) %all-gather.7.cloned.1.call-update) | async-done | bytes 2097168 | tf_op jit(solution)/shard_map/all_gather | solution.py:117
  369.9 1.7 fusion.227
  371.7 347.5 %all-gather.9.cloned.1.call-done = bf16[4096,256]{1,0:T(8,128)(2,1)} async-done(((bf16[64,256]{1,0:T(8,128)(2,1)}), bf16[4096,256]{1,0:T(8,128)(2,1)}) %all-gather.9.cloned.1.call-update) | async-done | bytes 2097168 | tf_op jit(solution)/shard_map/all_gather | solution.py:118
  719.3 2.6 fusion.226
  721.9 2.1 copy.236
  724.0 2.0 copy.233
  727.9 1.5 bitcast_reduce_fusion.10
  729.3 1.5 bitcast_reduce_fusion.9
  730.8 1.5 bitcast_reduce_fusion.8
  732.3 1.5 bitcast_reduce_fusion.11
  733.8 3.2 fusion.152
  737.1 3.0 fusion.148
  740.1 2.3 fusion.197
  742.4 2.1 fusion.191
  744.6 2.1 fusion.185
  746.7 3.0 fusion.179
  749.7 250.1 %all-gather.5.cloned.1.call-done = bf16[8192,256]{0,1:T(8,128)(2,1)} async-done(((bf16[128,256]{0,1:T(8,128)(2,1)}), bf16[8192,256]{0,1:T(8,128)(2,1)}) %all-gather.5.cloned.1.call-update) | async-done | bytes 4194320 | tf_op jit(solution)/shard_map/all_gather | solution.py:130
  999.8 280.6 %all-gather.11.cloned.1.call-done = bf16[8192,256]{0,1:T(8,128)(2,1)} async-done(((bf16[128,256]{0,1:T(8,128)(2,1)}), bf16[8192,256]{0,1:T(8,128)(2,1)}) %all-gather.11.cloned.1.call-update) | async-done | bytes 4194320 | tf_op jit(solution)/shard_map/all_gather | solution.py:131
  1280.3 72.9 %conditional.1 = (f32[2,6,128]{2,1,0:T(8,128)S(1)}, f32[128,2,6,128]{0,3,2,1:T(8,128)S(1)}) conditional(s32[]{:T(128)} %convert_element_type.45, (s32[8192]{0:T(1024)S(1)}, s32[]{:T(128)}, bf16[8192,256]{0,1:T(8,128)(2,1)}, bf16[128,2,6,128]{0,3,2,1:T(8,128)(2,1)S(1)}, f32[2,6,128]{2,1,0:T(8,128)S(1)}, /*index=5*/f32[2,6,128]{2,1,0:T(8,128)S(1)}, ...), branch_computations={%region_10.27_spmd, %region_27.28_spmd} | conditional | flops 6584163840 | bytes 311802944 | solution.py:100
  1280.3 5.7 fusion.223
  1286.2 1.5 bitcast_reduce_fusion.7
  1287.6 1.5 bitcast_reduce_fusion
  1289.1 1.5 bitcast_reduce_fusion.1
  1290.6 1.5 bitcast_reduce_fusion.2
  1292.0 1.5 bitcast_reduce_fusion.3
  1293.5 1.5 bitcast_reduce_fusion.4
  1295.0 4.5 bitcast_reduce_fusion.5
  1299.5 4.0 bitcast_reduce_fusion.6
  1304.2 2.2 fusion.9
  1306.4 3.7 fusion.11
  1310.2 1.8 fusion.13
  1312.0 1.8 fusion.15
  1313.8 1.8 fusion.17
  1315.6 1.8 fusion.19
  1317.4 1.8 fusion.21
  1319.2 1.9 fusion.23
  1321.9 4.6 fusion.114
  1326.5 6.0 fusion.108
  1332.6 5.9 fusion.102
  1338.6 4.2 fusion.96
  1342.8 3.3 fusion.90
  1346.1 2.3 fusion.84
  1348.5 2.1 fusion.78
  1350.6 2.1 fusion.72
  (135 shorter events, 10.1 us)
Async XLA Ops:
  6.5 363.3 %all-gather.7.cloned.1.call-start = ((), (), s32[]{:S(2)}) async-start(), calls=%async_computation.3 | async-start | bytes 2129920 | tf_op jit(solution)/shard_map/all_gather | solution.py:117
  23.5 695.7 %all-gather.9.cloned.1.call-start = ((), (), s32[]{:S(2)}) async-start(), calls=%async_computation.4 | async-start | bytes 2129920 | tf_op jit(solution)/shard_map/all_gather | solution.py:118
  35.2 964.5 %all-gather.5.cloned.1.call-start = ((), (), s32[]{:S(2)}) async-start(), calls=%async_computation.2 | async-start | bytes 4259840 | tf_op jit(solution)/shard_map/all_gather | solution.py:130
  36.9 1243.4 %all-gather.11.cloned.1.call-start = ((), (), s32[]{:S(2)}) async-start(), calls=%async_computation.5 | async-start | bytes 4259840 | tf_op jit(solution)/shard_map/all_gather | solution.py:131
  42.8 685.1 %copy-start.29 = (pred[1024]{0:T(1024)(128)(4,1)}, pred[1024]{0:T(1024)(128)(4,1)S(1)}, u32[]{:S(2)}) copy-start(pred[1024]{0:T(1024)(128)(4,1)S(1)} %get-tuple-element.181) | copy-start | bytes 3076
  42.8 689.5 %copy-start.31 = (pred[1024]{0:T(1024)(128)(4,1)}, pred[1024]{0:T(1024)(128)(4,1)S(1)}, u32[]{:S(2)}) copy-start(pred[1024]{0:T(1024)(128)(4,1)S(1)} %get-tuple-element.178) | copy-start | bytes 3076
  42.8 691.0 %copy-start.25 = (pred[1024]{0:T(1024)(128)(4,1)}, pred[1024]{0:T(1024)(128)(4,1)S(1)}, u32[]{:S(2)}) copy-start(pred[1024]{0:T(1024)(128)(4,1)S(1)} %get-tuple-element.179) | copy-start | bytes 3076
  42.8 691.0 %copy-start.27 = (pred[1024]{0:T(1024)(128)(4,1)}, pred[1024]{0:T(1024)(128)(4,1)S(1)}, u32[]{:S(2)}) copy-start(pred[1024]{0:T(1024)(128)(4,1)S(1)} %get-tuple-element.180) | copy-start | bytes 3076
  733.8 3.2 copy-start.30
  733.8 3.2 copy-start.32
  740.1 2.3 copy-start.9
  742.4 2.1 copy-start.8
  742.4 2.1 copy-start.28
  744.5 2.2 copy-start.7
  744.5 2.2 copy-start.26
  1286.1 18.1 %copy-start.24 = (pred[1024]{0:T(1024)(128)(4,1)}, pred[1024]{0:T(1024)(128)(4,1)S(1)}, u32[]{:S(2)}) copy-start(pred[1024]{0:T(1024)(128)(4,1)S(1)} %get-tuple-element.131) | copy-start | bytes 3076 | tf_op jit(solution)/shard_map/cond
  1286.1 20.3 %copy-start.22 = (pred[1024]{0:T(1024)(128)(4,1)}, pred[1024]{0:T(1024)(128)(4,1)S(1)}, u32[]{:S(2)}) copy-start(pred[1024]{0:T(1024)(128)(4,1)S(1)} %get-tuple-element.138) | copy-start | bytes 3076 | tf_op jit(solution)/shard_map/cond
  1286.1 24.0 %copy-start.20 = (pred[1024]{0:T(1024)(128)(4,1)}, pred[1024]{0:T(1024)(128)(4,1)S(1)}, u32[]{:S(2)}) copy-start(pred[1024]{0:T(1024)(128)(4,1)S(1)} %get-tuple-element.137) | copy-start | bytes 3076 | tf_op jit(solution)/shard_map/cond
  1286.1 25.8 %copy-start.18 = (pred[1024]{0:T(1024)(128)(4,1)}, pred[1024]{0:T(1024)(128)(4,1)S(1)}, u32[]{:S(2)}) copy-start(pred[1024]{0:T(1024)(128)(4,1)S(1)} %get-tuple-element.136) | copy-start | bytes 3076 | tf_op jit(solution)/shard_map/cond
  1286.1 27.6 %copy-start.16 = (pred[1024]{0:T(1024)(128)(4,1)}, pred[1024]{0:T(1024)(128)(4,1)S(1)}, u32[]{:S(2)}) copy-start(pred[1024]{0:T(1024)(128)(4,1)S(1)} %get-tuple-element.135) | copy-start | bytes 3076 | tf_op jit(solution)/shard_map/cond
  1286.1 29.4 %copy-start.14 = (pred[1024]{0:T(1024)(128)(4,1)}, pred[1024]{0:T(1024)(128)(4,1)S(1)}, u32[]{:S(2)}) copy-start(pred[1024]{0:T(1024)(128)(4,1)S(1)} %get-tuple-element.134) | copy-start | bytes 3076 | tf_op jit(solution)/shard_map/cond
  1286.1 31.2 %copy-start.12 = (pred[1024]{0:T(1024)(128)(4,1)}, pred[1024]{0:T(1024)(128)(4,1)S(1)}, u32[]{:S(2)}) copy-start(pred[1024]{0:T(1024)(128)(4,1)S(1)} %get-tuple-element.133) | copy-start | bytes 3076 | tf_op jit(solution)/shard_map/cond
  1286.1 33.0 %copy-start.10 = (pred[1024]{0:T(1024)(128)(4,1)}, pred[1024]{0:T(1024)(128)(4,1)S(1)}, u32[]{:S(2)}) copy-start(pred[1024]{0:T(1024)(128)(4,1)S(1)} %get-tuple-element.132) | copy-start | bytes 3076 | tf_op jit(solution)/shard_map/cond
  1287.6 16.6 %copy-start = (f32[2,1024,128,6]{2,1,3,0:T(8,128)}, f32[2,1024,128,6]{2,1,3,0:T(8,128)S(1)}, u32[]{:S(2)}) copy-start(f32[2,1024,128,6]{2,1,3,0:T(8,128)S(1)} %get-tuple-element.154) | copy-start | bytes 18874372 | tf_op jit(solution)/shard_map/cond
  1295.0 17.0 %copy-start.1 = (f32[2,1024,128,6]{2,1,3,0:T(8,128)}, f32[2,1024,128,6]{2,1,3,0:T(8,128)S(1)}, u32[]{:S(2)}) copy-start(f32[2,1024,128,6]{2,1,3,0:T(8,128)S(1)} %get-tuple-element.148) | copy-start | bytes 18874372 | tf_op jit(solution)/shard_map/cond
  1304.2 6.0 slice-start.4
  1304.2 5.9 slice-start.5
  1315.6 6.3 slice-start
  1317.4 4.4 slice-start.1
  1321.8 4.6 copy-start.23
  1321.8 4.6 copy-start.38
  1326.4 6.1 copy-start.6
  1326.4 6.1 copy-start.21
  1326.4 6.1 copy-start.37
  1326.5 12.1 slice-start.2
  1332.5 6.0 copy-start.5
  1332.5 6.0 copy-start.19
  1332.5 6.0 copy-start.36
  1332.5 6.0 slice-start.3
  1338.5 4.2 copy-start.4
  1338.5 4.2 copy-start.17
  1338.5 4.2 copy-start.35
  1342.7 3.4 copy-start.3
  1342.7 3.4 copy-start.15
  1342.7 3.4 copy-start.34
  1346.0 2.4 copy-start.2
  1346.1 2.4 copy-start.13
  1346.1 2.4 copy-start.33
  (1 other events, 2.1 us)
Sparse Core Ops, SparseCore 0:
  23.6 346.1 all-gather.6
  371.7 347.5 all-gather.8
  721.0 278.7 all-gather.4
  1001.4 278.9 all-gather.10
where the time goes:
time: 1370 us; the launch traced here: 1360 us
  waiting for transfers between devices  1210 us (88%)
  matrix products  63.2 us (5%)
  blocking collectives  27.1 us (2%)
  other arithmetic  25.5 us (2%)
  local copies, waits for them, and re-layouts  24.7 us (2%)
  between operations  14.4 us (1%)
    all_gather x1, waiting for transfers between devices, on_device(): value_piece = lax.all_gather(cache_v, 'stretch', axis=0, tiled=True)  348 us
    all_gather x1, waiting for transfers between devices, on_device(): key_piece = lax.all_gather(cache_k, 'stretch', axis=0, tiled=True)  327 us
    all_gather x1, waiting for transfers between devices, on_device(): lax.all_gather(values, 'stretch', axis=0, tiled=True)  281 us
    all_gather x1, waiting for transfers between devices, on_device(): lax.all_gather(keys, 'stretch', axis=0, tiled=True)  250 us
    dot_general x12, matrix products, absorb(): jnp.einsum('kgqt,tkd->qkgd', weights.astype(jnp.bfloat16), values_split,...  40.1 us
  transfers between devices with their start and end apart: 4, of which 4 were waited for; matrix products, arithmetic and copies ran while one was open for 3% of the time, Pallas kernels for 0%

commit v1 on v0

v1 whole, which is shorter than its diff:
```python
import functools

import jax
import jax.numpy as jnp
from jax import lax
from jax.experimental import pallas as pl
from jax.experimental.pallas import tpu as pltpu
from jax.sharding import Mesh, PartitionSpec as P

D = 128
GROUP = 6
WIDE = GROUP * D
HALF = 64
CROWS = 32
BLOCK = HALF + CROWS
ROWS = GROUP * HALF
NEG = -1e30
LOG2E = 1.4426950408889634
SCALE = D**-0.5 * LOG2E
KEYS = 512

VMEM = pltpu.VMEM
ANY = pl.ANY


def params(mib):
    return pltpu.CompilerParams(vmem_limit_bytes=mib * 2**20)


def slot():
    return 2 * (lax.axis_index("x") & 1) + lax.axis_index("core")


def cut_body(q_ref, k_ref, v_ref, ck_ref, cv_ref, *outs):
    q_out, kv_out, send_ref, own_ref = outs[:4], outs[4:8], outs[8], outs[9]
    x = lax.axis_index("x")
    half = lax.axis_index("zh")
    for s in range(4):
        piece = x ^ s
        rows = pl.ds(pl.multiple_of((piece & 1) * HALF, HALF), HALF)
        head = piece >> 1
        narrow = pl.ds(pl.multiple_of(head * D, D), D)
        kv_out[s][:, :D] = k_ref[rows, narrow]
        kv_out[s][:, D:] = v_ref[rows, narrow]
        q_out[s][...] = q_ref[rows, pl.ds(pl.multiple_of(head * WIDE, D), WIDE)]
    mine = pl.ds(pl.multiple_of(half * 4 * D, D), 4 * D)
    other = pl.ds(pl.multiple_of((1 - half) * 4 * D, D), 4 * D)
    own_ref[:, : 4 * D] = ck_ref[:, mine]
    own_ref[:, 4 * D :] = cv_ref[:, mine]
    send_ref[:, : 4 * D] = ck_ref[:, other]
    send_ref[:, 4 * D :] = cv_ref[:, other]


def cut(q, k, v, ck, cv):
    bf = jnp.bfloat16
    return pl.pallas_call(
        cut_body,
        out_shape=[jax.ShapeDtypeStruct((HALF, WIDE), bf)] * 4
        + [jax.ShapeDtypeStruct((HALF, 2 * D), bf)] * 4
        + [jax.ShapeDtypeStruct((16, 8 * D), bf)] * 2,
        name="cut",
    )(q, k, v, ck, cv)


def cut_cache_body(own_ref, got_ref, *outs):
    x = lax.axis_index("x")
    for s in range(4):
        head = (x + s) & 3
        for part, ref in enumerate((own_ref, got_ref)):
            rows = slice(16 * part, 16 * part + 16)
            outs[s][rows, :D] = ref[:, pl.ds(pl.multiple_of(head * D, D), D)]
            outs[s][rows, D:] = ref[:, pl.ds(pl.multiple_of((head + 4) * D, D), D)]


def cut_cache(own, got):
    return pl.pallas_call(
        cut_cache_body,
        out_shape=[jax.ShapeDtypeStruct((CROWS, 2 * D), jnp.bfloat16)] * 4,
        name="cut_cache",
    )(own, got)


def join_body(*refs):
    kv, cache, out = refs[:4], refs[4:8], refs[8]
    x = lax.axis_index("x")
    r = slot()
    for s in range(4):
        out[pl.ds(r ^ s, 1), :HALF, :] = kv[s][...][None]
        out[pl.ds((x + 4 - s) & 3, 1), HALF:, :] = cache[s][...][None]


def join(kv, cache):
    return pl.pallas_call(
        join_body,
        out_shape=jax.ShapeDtypeStruct((4, BLOCK, 2 * D), jnp.bfloat16),
        name="join",
    )(*kv, *cache)


def place_body(*refs):
    pieces, out = refs[:4], refs[4]
    x = lax.axis_index("x")
    for s in range(4):
        piece = x ^ s
        rows = pl.ds(pl.multiple_of((piece & 1) * HALF, HALF), HALF)
        out[rows, pl.ds(pl.multiple_of((piece >> 1) * WIDE, D), WIDE)] = pieces[s][...]


def place(pieces):
    return pl.pallas_call(
        place_body,
        out_shape=jax.ShapeDtypeStruct((2 * HALF, 2 * WIDE), jnp.bfloat16),
        name="place",
    )(*pieces)


def attend_body(owner_ref, window_ref, *refs):
    q_in, blocks, outs = refs[:4], refs[4:14], refs[14:18]
    fresh, paged, sorted_kv, q_all, acc, top, sem = refs[18:]
    r = slot()
    zl, y, core = lax.axis_index("zl"), lax.axis_index("y"), lax.axis_index("core")

    copies = []

    def bring(source, first, depth, ysrc, csrc):
        for i in range(depth):
            zsrc = (zl + 4 - (first + i)) & 3
            chip = zsrc * 4 + ysrc
            n = len(copies)
            one = pltpu.make_async_copy(
                source.at[i, :, :HALF, :],
                fresh.at[:, pl.ds(pl.multiple_of((chip * 2 + csrc) * HALF, HALF), HALF), :],
                sem.at[2 * n],
            )
            two = pltpu.make_async_copy(
                source.at[i, :, HALF:, :],
                paged.at[:, chip, pl.ds(pl.multiple_of(csrc * CROWS, CROWS), CROWS), :],
                sem.at[2 * n + 1],
            )
            one.start()
            two.start()
            copies.append((one, two))

    for which in range(2):
        c = core if which == 0 else 1 - core
        b = blocks[5 * which : 5 * which + 5]
        bring(b[0], 0, 4, y, c)
        bring(b[1], 0, 4, (y + 3) & 3, c)
        bring(b[2], 0, 4, (y + 1) & 3, c)
        bring(b[3], 0, 2, (y + 2) & 3, c)
        bring(b[4], 2, 2, (y + 2) & 3, c)

    for s in range(4):
        for g in range(GROUP):
            row = pl.multiple_of((r ^ s) * ROWS + g * HALF, HALF)
            q_all[pl.ds(row, HALF), :] = q_in[s][:, g * D : (g + 1) * D]
    acc[...] = jnp.zeros_like(acc)
    top[...] = jnp.full_like(top, NEG)
    for one, two in copies:
        one.wait()
        two.wait()

    ones = jnp.ones((KEYS, D), jnp.bfloat16)

    def step(c, kv):
        rows = slice(c * ROWS, (c + 1) * ROWS)
        k = kv[:, :D]
        v = jnp.concatenate([kv[:, D:], ones], axis=1)
        s = lax.dot_general(
            q_all[rows, :], k, (((1,), (1,)), ((), ())), preferred_element_type=jnp.float32
        )
        old = top[rows, :]
        new = jnp.maximum(old, jnp.max(s, axis=1, keepdims=True))
        p = jnp.exp2((s - new[:, :1]) * SCALE).astype(jnp.bfloat16)
        update = lax.dot_general(
            p, v, (((1,), (0,)), ((), ())), preferred_element_type=jnp.float32
        )
        factor = jnp.exp2((old - new) * SCALE)
        acc[rows, :D] = acc[rows, :D] * factor + update[:, :D]
        acc[rows, D:] = acc[rows, D:] * factor + update[:, D:]
        top[rows, :] = new

    for t in range(4):

        def fresh_step(i, carry, t=t):
            kv = fresh[t, pl.ds(pl.multiple_of(i * KEYS, KEYS), KEYS), :]
            for c in range(t, 4):
                step(c, kv)
            return carry

        lax.fori_loop(0, 2048 // KEYS, fresh_step, 0)

    pages = KEYS // 64
    for cached in range(2):

        def sort_step(i, carry, cached=cached):
            page = owner_ref[cached * 32 + i]
            sorted_kv[pl.ds(pl.multiple_of(i * 64, 64), 64), :] = paged[page >> 4, page & 15]
            return carry

        lax.fori_loop(0, 32, sort_step, 0)

        def cache_step(i, carry, c):
            step(c, sorted_kv[pl.ds(pl.multiple_of(i * KEYS, KEYS), KEYS), :])
            return carry

        for c in range(4):
            if cached == 1:
                lax.fori_loop(0, 2048 // KEYS, functools.partial(cache_step, c=c), 0)
            else:

                @pl.when(window_ref[c] > 1)
                def _(c=c):
                    lax.fori_loop(0, 2048 // KEYS, functools.partial(cache_step, c=c), 0)

    for s in range(4):
        for g in range(GROUP):
            row = pl.multiple_of((r ^ s) * ROWS + g * HALF, HALF)
            total = acc[pl.ds(row, HALF), :]
            outs[s][:, g * D : (g + 1) * D] = (total[:, :D] / total[:, D:]).astype(jnp.bfloat16)


def attend(owner, window, q, blocks):
    bf = jnp.bfloat16
    smem = pl.BlockSpec(memory_space=pltpu.SMEM)
    vmem = pl.BlockSpec(memory_space=VMEM)
    return pl.pallas_call(
        attend_body,
        in_specs=[smem, smem] + [vmem] * 4 + [pl.BlockSpec(memory_space=ANY)] * 10,
        out_specs=[vmem] * 4,
        out_shape=[jax.ShapeDtypeStruct((HALF, WIDE), bf)] * 4,
        scratch_shapes=[
            VMEM((4, 2048, 2 * D), bf),
            VMEM((4, 16, 64, 2 * D), bf),
            VMEM((2048, 2 * D), bf),
            VMEM((4 * ROWS, D), bf),
            VMEM((4 * ROWS, 2 * D), jnp.float32),
            VMEM((4 * ROWS, D), jnp.float32),
            pltpu.SemaphoreType.DMA((64,)),
        ],
        compiler_params=params(48),
        name="attend",
    )(owner, window, *q, *blocks)


def spread(s):
    pairs = []
    for x in range(4):
        for core in range(2):
            piece = x ^ s
            pairs.append((x * 2 + core, (2 * core + (piece >> 1)) * 2 + (piece & 1)))
    return pairs


def shift(array, axis, by, size=4):
    return lax.ppermute(array, axis, [(i, (i + by) % size) for i in range(size)])


def on_device(queries, keys, values, cache_keys, cache_values, page_owner, window):
    made = cut(queries, keys, values, cache_keys, cache_values)
    q_pieces, kv_pieces, send, own = made[:4], made[4:8], made[8], made[9]
    got = shift(send, "zh", 1, 2)
    kv = [lax.ppermute(kv_pieces[s], ("x", "core"), spread(s)) for s in range(4)]
    q = [lax.ppermute(q_pieces[s], ("x", "core"), spread(s)) for s in range(4)]
    cache_pieces = cut_cache(own, got)
    cache = [cache_pieces[0]] + [shift(cache_pieces[s], "x", s) for s in range(1, 4)]
    block = join(kv, cache)
    column = jnp.stack([block] + [shift(block, "zl", s) for s in range(1, 4)])
    up = shift(column, "y", 1)
    down = shift(column, "y", 3)
    far_a = shift(up[:2], "y", 1)
    far_b = shift(down[2:], "y", 3)
    mine = [column, up, down, far_a, far_b]
    theirs = [shift(part, "core", 1, 2) for part in mine]
    outs = attend(page_owner, window, q, mine + theirs)
    back = [
        lax.ppermute(outs[s], ("x", "core"), [(b, a) for a, b in spread(s)]) for s in range(4)
    ]
    return place(back)


def solution(mesh):
    fine = Mesh(mesh.devices.reshape(4, 4, 4, 2, 2), ("x", "zl", "y", "zh", "core"))
    tokens, heads = ("x", "zl", "y"), ("zh", "core")
    return jax.shard_map(
        on_device,
        mesh=fine,
        in_specs=(
            P(tokens, heads),
            P(tokens, heads),
            P(tokens, heads),
            P(tokens + heads, None),
            P(tokens + heads, None),
            P(),
            P(),
        ),
        out_specs=P(tokens, heads),
        check_vma=False,
    )
```

time: 1370 us -> 161 us (0.12)
  the two profiles are of different devices: /device:TPU:8 before, /device:TPU:1 now
where the time goes in v1:
time: 161 us; the launch traced here: 162 us
  Pallas kernels  62.6 us (39%)
  starting transfers between devices  57 us (35%)
  waiting for transfers between devices  38 us (24%)
  local copies, waits for them, and re-layouts  2.82 us (2%)
    pallas_call x1, Pallas kernels, attend(): pl.pallas_call(attend_body, in_specs=[smem, smem] + [vmem] * 4 + [pl.Bloc...  55.9 us
    ppermute x16, waiting for transfers between devices, shift(): lax.ppermute(array, axis, [(i, (i + by) % size) for i in range(size)])  35.2 us
    ppermute x16, starting transfers between devices, shift(): lax.ppermute(array, axis, [(i, (i + by) % size) for i in range(size)])  28 us
    ppermute x4, starting transfers between devices, on_device(): q = [lax.ppermute(q_pieces[s], ('x', 'core'), spread(s)) for s in range(4)]  10.5 us
    ppermute x4, starting transfers between devices, on_device(): lax.ppermute(outs[s], ('x', 'core'), [(b, a) for a, b in spread(s)])  9.73 us
    ppermute x4, starting transfers between devices, on_device(): lax.ppermute(kv_pieces[s], ('x', 'core'), spread(s))  8.76 us
  transfers between devices with their start and end apart: 28, of which 10 were waited for; matrix products, arithmetic and copies ran while one was open for 0% of the time, Pallas kernels for 1%

profile of v1, /device:TPU:1, one launch (start us, length us, event | category | flops | bytes accessed | tf_op | source)
XLA Modules:
  0.0 161.8 jit_solution(11560904959059674882)
XLA Ops:
  0.0 1.9 %cut.1 = (bf16[64,768]{1,0:T(8,128)(2,1)}, bf16[64,768]{1,0:T(8,128)(2,1)}, bf16[64,768]{1,0:T(8,128)(2,1)}, bf16[64,768]{1,0:T(8,128)(2,1)}, bf16[64,256]{1,0:T...) custom-call(bf16[128,1536]{1,0:T(8,128)(2,1)} %q_ref.1, ...), custom_call_target="tpu_custom_call" | custom-call | tf_op jit(solution)/shard_map/cut/pallas_call | solution.py:56
  1.9 7.8 %collective-permute-start.8 = (bf16[16,1024]{1,0:T(8,128)(2,1)}, bf16[16,1024]{1,0:T(8,128)(2,1)S(1)}, u32[]{:S(2)}, u32[]{:S(2)}) collective-permute-start(bf16[16,1024]{1,0:T(8,128)(2,1)} %get-tuple-element.32), channel_id=1, source_target_pairs={{0,2},{2,0},{1,3},{3,1},{4,6},{6,4},{5,7},{7,5},{8,10},{10,8},{9,1... | collective-permute-start | bytes 98312 | tf_op jit(solution)/shard_map/ppermute | solution.py:256
  9.8 5.5 %collective-permute-start.4 = (bf16[64,256]{1,0:T(8,128)(2,1)}, bf16[64,256]{1,0:T(8,128)(2,1)S(1)}, u32[]{:S(2)}, u32[]{:S(2)}) collective-permute-start(bf16[64,256]{1,0:T(8,128)(2,1)} %get-tuple-element.27), channel_id=1, source_target_pairs={{0,0},{1,128},{64,1},{65,129},{128,64},{129,192},{192,65},{193,193... | collective-permute-start | bytes 98312 | tf_op jit(solution)/shard_map/ppermute | solution.py:263
  15.2 1.0 collective-permute-start.5
  16.2 0.2 collective-permute-start.6
  16.5 2.0 %collective-permute-start.7 = (bf16[64,256]{1,0:T(8,128)(2,1)}, bf16[64,256]{1,0:T(8,128)(2,1)S(1)}, u32[]{:S(2)}, u32[]{:S(2)}) collective-permute-start(bf16[64,256]{1,0:T(8,128)(2,1)} %get-tuple-element.30), channel_id=1, source_target_pairs={{0,65},{1,193},{64,64},{65,192},{128,1},{129,129},{192,0},{193,128... | collective-permute-start | bytes 98312 | tf_op jit(solution)/shard_map/ppermute | solution.py:263
  18.5 0.6 copy-done.12
  19.2 1.4 cut_cache.1
  20.6 3.2 %collective-permute-start.9 = (bf16[32,256]{1,0:T(8,128)(2,1)}, bf16[32,256]{1,0:T(8,128)(2,1)S(1)}, u32[]{:S(2)}, u32[]{:S(2)}) collective-permute-start(bf16[32,256]{1,0:T(8,128)(2,1)} %get-tuple-element.34), channel_id=1, source_target_pairs={{0,64},{64,128},{128,192},{192,0},{1,65},{65,129},{129,193},{193,1... | collective-permute-start | bytes 49160 | tf_op jit(solution)/shard_map/ppermute | solution.py:256
  23.7 0.7 collective-permute-start.10
  24.4 1.8 %collective-permute-start.11 = (bf16[32,256]{1,0:T(8,128)(2,1)}, bf16[32,256]{1,0:T(8,128)(2,1)S(1)}, u32[]{:S(2)}, u32[]{:S(2)}) collective-permute-start(bf16[32,256]{1,0:T(8,128)(2,1)} %get-tuple-element.36), channel_id=1, source_target_pairs={{0,192},{64,0},{128,64},{192,128},{1,193},{65,1},{129,65},{193,129... | collective-permute-start | bytes 49160 | tf_op jit(solution)/shard_map/ppermute | solution.py:256
  26.3 1.8 %collective-permute-done.10.refs_6_ = bf16[32,256]{1,0:T(8,128)(2,1)S(1)} collective-permute-done((bf16[32,256]{1,0:T(8,128)(2,1)}, bf16[32,256]{1,0:T(8,128)(2,1)S(1)}, u32[]{:S(2)}, u32[]{:S(2)}) %collective-permute-start.10) | collective-permute-done | bytes 16416 | tf_op jit(solution)/shard_map/ppermute | solution.py:256
  28.1 0.5 copy-done.14
  28.6 0.0 copy-done.15
  28.7 1.5 join.1
  30.2 1.6 %collective-permute-start.14 = (bf16[4,96,256]{2,1,0:T(8,128)(2,1)}, bf16[4,96,256]{2,1,0:T(8,128)(2,1)S(1)}, u32[]{:S(2)}, u32[]{:S(2)}) collective-permute-start(bf16[4,96,256]{2,1,0:T(8,128)(2,1)} %join.1), channel_id=1, source_target_pairs={{0,48},{16,0},{32,16},{48,32},{1,49},{17,1},{33,17},{49,33},{2,50}... | collective-permute-start | bytes 589832 | tf_op jit(solution)/shard_map/ppermute | solution.py:256
  31.8 0.3 collective-permute-start.13
  32.1 0.7 collective-permute-start.12
  32.9 3.0 %collective-permute-done.14 = bf16[4,96,256]{2,1,0:T(8,128)(2,1)S(1)} collective-permute-done((bf16[4,96,256]{2,1,0:T(8,128)(2,1)}, bf16[4,96,256]{2,1,0:T(8,128)(2,1)S(1)}, u32[]{:S(2)}, u32[]{:S(2)}) %collective-permute-start.14) | collective-permute-done | bytes 196640 | tf_op jit(solution)/shard_map/ppermute | solution.py:256
  35.9 13.1 %collective-permute-done.13 = bf16[4,96,256]{2,1,0:T(8,128)(2,1)S(1)} collective-permute-done((bf16[4,96,256]{2,1,0:T(8,128)(2,1)}, bf16[4,96,256]{2,1,0:T(8,128)(2,1)S(1)}, u32[]{:S(2)}, u32[]{:S(2)}) %collective-permute-start.13) | collective-permute-done | bytes 196640 | tf_op jit(solution)/shard_map/ppermute | solution.py:256
  49.0 1.1 pad_maximum_fusion.refs_4_
  50.1 2.8 %collective-permute-start.16 = (bf16[4,4,96,256]{3,2,1,0:T(8,128)(2,1)S(1)}, bf16[4,4,96,256]{3,2,1,0:T(8,128)(2,1)S(1)}, u32[]{:S(2)}, u32[]{:S(2)}) collective-permute-start(bf16[4,4,96,256]{3,2,1,0:T(8,128)(2,1)S(1)} %pad_maximum_fusion.refs_4_), channel_id=1, source_target_pairs={{0,12},{4,0},{8,4},{12,8},{1,13},{5,1},{9,5},{13,9},{2,14},{6,2},{... | collective-permute-start | bytes 2359304 | tf_op jit(solution)/shard_map/ppermute | solution.py:256
  52.9 5.6 %collective-permute-start = (bf16[64,768]{1,0:T(8,128)(2,1)S(1)}, bf16[64,768]{1,0:T(8,128)(2,1)S(1)}, u32[]{:S(2)}, u32[]{:S(2)}) collective-permute-start(bf16[64,768]{1,0:T(8,128)(2,1)S(1)} %copy-done.19), channel_id=1, source_target_pairs={{0,0},{1,128},{64,1},{65,129},{128,64},{129,192},{192,65},{193,193... | collective-permute-start | bytes 294920 | tf_op jit(solution)/shard_map/ppermute | solution.py:264
  58.6 1.7 %collective-permute-start.1 = (bf16[64,768]{1,0:T(8,128)(2,1)S(1)}, bf16[64,768]{1,0:T(8,128)(2,1)S(1)}, u32[]{:S(2)}, u32[]{:S(2)}) collective-permute-start(bf16[64,768]{1,0:T(8,128)(2,1)S(1)} %copy-done.18), channel_id=1, source_target_pairs={{0,1},{1,129},{64,0},{65,128},{128,65},{129,193},{192,64},{193,192... | collective-permute-start | bytes 294920 | tf_op jit(solution)/shard_map/ppermute | solution.py:264
  60.3 7.6 %collective-permute-done.16.refs_6_ = bf16[4,4,96,256]{3,2,1,0:T(8,128)(2,1)S(1)} collective-permute-done((bf16[4,4,96,256]{3,2,1,0:T(8,128)(2,1)S(1)}, bf16[4,4,96,256]{3,2,1,0:T(8,128)(2,1)S(1)}, u32[]{:S(2)}, u32[]{:S(2)}) %collective-permute-start.16) | collective-permute-done | bytes 786464 | tf_op jit(solution)/shard_map/ppermute | solution.py:256
  67.9 3.2 %collective-permute-start.3 = (bf16[64,768]{1,0:T(8,128)(2,1)S(1)}, bf16[64,768]{1,0:T(8,128)(2,1)S(1)}, u32[]{:S(2)}, u32[]{:S(2)}) collective-permute-start(bf16[64,768]{1,0:T(8,128)(2,1)S(1)} %copy-done.16), channel_id=1, source_target_pairs={{0,65},{1,193},{64,64},{65,192},{128,1},{129,129},{192,0},{193,128... | collective-permute-start | bytes 294920 | tf_op jit(solution)/shard_map/ppermute | solution.py:264
  71.1 0.0 copy-start
  71.2 0.0 copy-start.1
  71.2 2.9 %collective-permute-start.19 = (bf16[4,4,96,256]{3,2,1,0:T(8,128)(2,1)S(1)}, bf16[4,4,96,256]{3,2,1,0:T(8,128)(2,1)S(1)}, u32[]{:S(2)}, u32[]{:S(2)}) collective-permute-start(bf16[4,4,96,256]{3,2,1,0:T(8,128)(2,1)S(1)} %pad_maximum_fusion.refs_4_), channel_id=1, source_target_pairs={{0,1},{1,0},{2,3},{3,2},{4,5},{5,4},{6,7},{7,6},{8,9},{9,8},{10,11... | collective-permute-start | bytes 2359304 | tf_op jit(solution)/shard_map/ppermute | solution.py:256
  74.1 2.2 %collective-permute-start.18 = (bf16[2,4,96,256]{3,2,1,0:T(8,128)(2,1)S(1)}, bf16[2,4,96,256]{3,2,1,0:T(8,128)(2,1)S(1)}, u32[]{:S(2)}, u32[]{:S(2)}) collective-permute-start(bf16[2,4,96,256]{3,2,1,0:T(8,128)(2,1)S(1)} %slice.9), channel_id=1, source_target_pairs={{0,12},{4,0},{8,4},{12,8},{1,13},{5,1},{9,5},{13,9},{2,14},{6,2},{... | collective-permute-start | bytes 1179656 | tf_op jit(solution)/shard_map/ppermute | solution.py:256
  76.3 0.4 collective-permute-start.21
  76.7 0.4 collective-permute-done.3.refs_3_
  77.1 1.7 %collective-permute-start.20 = (bf16[4,4,96,256]{3,2,1,0:T(8,128)(2,1)S(1)}, bf16[4,4,96,256]{3,2,1,0:T(8,128)(2,1)S(1)}, u32[]{:S(2)}, u32[]{:S(2)}) collective-permute-start(bf16[4,4,96,256]{3,2,1,0:T(8,128)(2,1)S(1)} %collective-permute-done.15.refs_5_), channel_id=1, source_target_pairs={{0,1},{1,0},{2,3},{3,2},{4,5},{5,4},{6,7},{7,6},{8,9},{9,8},{10,11... | collective-permute-start | bytes 2359304 | tf_op jit(solution)/shard_map/ppermute | solution.py:256
  78.8 6.1 %collective-permute-done.18.refs_8_ = bf16[2,4,96,256]{3,2,1,0:T(8,128)(2,1)S(1)} collective-permute-done((bf16[2,4,96,256]{3,2,1,0:T(8,128)(2,1)S(1)}, bf16[2,4,96,256]{3,2,1,0:T(8,128)(2,1)S(1)}, u32[]{:S(2)}, u32[]{:S(2)}) %collective-permute-start.18) | collective-permute-done | bytes 393248 | tf_op jit(solution)/shard_map/ppermute | solution.py:256
  84.9 0.8 collective-permute-start.23
  85.7 2.2 %collective-permute-done.17.refs_7_ = bf16[2,4,96,256]{3,2,1,0:T(8,128)(2,1)S(1)} collective-permute-done((bf16[2,4,96,256]{3,2,1,0:T(8,128)(2,1)S(1)}, bf16[2,4,96,256]{3,2,1,0:T(8,128)(2,1)S(1)}, u32[]{:S(2)}, u32[]{:S(2)}) %collective-permute-start.17) | collective-permute-done | bytes 393248 | tf_op jit(solution)/shard_map/ppermute | solution.py:256
  87.9 1.1 collective-permute-start.22
  89.0 1.3 collective-permute-done.22.refs_12_
  90.4 0.9 copy-done.3
  91.3 55.9 %attend.1 = (bf16[64,768]{1,0:T(8,128)(2,1)S(1)}, bf16[64,768]{1,0:T(8,128)(2,1)S(1)}, bf16[64,768]{1,0:T(8,128)(2,1)S(1)}, bf16[64,768]{1,0:T(8,128)(2,1)S(1)}) custom-call(s32[64]{0:T(128)S(1)} %copy-done, s32[4]{0:T(128)S(1)} %copy-done.1, bf16[64,768]{1,0:T(8,128)(2,1)S(1)} %collective-permute-done.refs_0_, ...), custom_call_target="tpu_custom_call" | custom-call | tf_op jit(solution)/shard_map/attend/pallas_call | solution.py:227
  147.2 4.4 %collective-permute-start.24 = (bf16[64,768]{1,0:T(8,128)(2,1)S(1)}, bf16[64,768]{1,0:T(8,128)(2,1)S(1)}, u32[]{:S(2)}, u32[]{:S(2)}) collective-permute-start(bf16[64,768]{1,0:T(8,128)(2,1)S(1)} %get-tuple-element.37), channel_id=1, source_target_pairs={{0,0},{128,1},{1,64},{129,65},{64,128},{192,129},{65,192},{193,193... | collective-permute-start | bytes 294920 | tf_op jit(solution)/shard_map/ppermute | solution.py:277
  151.6 0.1 collective-permute-start.25
  151.7 0.8 collective-permute-start.26
  152.5 4.4 %collective-permute-start.27 = (bf16[64,768]{1,0:T(8,128)(2,1)S(1)}, bf16[64,768]{1,0:T(8,128)(2,1)S(1)}, u32[]{:S(2)}, u32[]{:S(2)}) collective-permute-start(bf16[64,768]{1,0:T(8,128)(2,1)S(1)} %get-tuple-element.40), channel_id=1, source_target_pairs={{65,0},{193,1},{64,64},{192,65},{1,128},{129,129},{0,192},{128,193... | collective-permute-start | bytes 294920 | tf_op jit(solution)/shard_map/ppermute | solution.py:277
  157.0 0.7 collective-permute-done.26.refs_2_
  157.7 1.7 %collective-permute-done.27.refs_3_ = bf16[64,768]{1,0:T(8,128)(2,1)S(1)} collective-permute-done((bf16[64,768]{1,0:T(8,128)(2,1)S(1)}, bf16[64,768]{1,0:T(8,128)(2,1)S(1)}, u32[]{:S(2)}, u32[]{:S(2)}) %collective-permute-start.27) | collective-permute-done | bytes 98336 | tf_op jit(solution)/shard_map/ppermute | solution.py:277
  159.4 0.6 copy-done.7
  160.0 1.8 %place.1 = bf16[128,1536]{1,0:T(8,128)(2,1)} custom-call(bf16[64,768]{1,0:T(8,128)(2,1)} %copy-done.4, bf16[64,768]{1,0:T(8,128)(2,1)} %copy-done.5, bf16[64,768]{1,0:T(8,128)(2,1)} %copy-done.6, bf16[64,768]{1,0:T(8,128)(2,1)} %copy-done.7), custom_call_target="tpu_custom_call" | custom-call | tf_op jit(solution)/shard_map/place/pallas_call | solution.py:110
  (56 shorter events, 0.2 us)
Async XLA Ops:
  1.9 16.6 %collective-permute-start.8 = (bf16[16,1024]{1,0:T(8,128)(2,1)}, bf16[16,1024]{1,0:T(8,128)(2,1)S(1)}, u32[]{:S(2)}, u32[]{:S(2)}) collective-permute-start(bf16[16,1024]{1,0:T(8,128)(2,1)} %get-tuple-element.32), channel_id=1, source_target_pairs={{0,2},{2,0},{1,3},{3,1},{4,6},{6,4},{5,7},{7,5},{8,10},{10,8},{9,1... | collective-permute-start | bytes 98312 | tf_op jit(solution)/shard_map/ppermute | solution.py:256
  9.8 14.0 %collective-permute-start.4 = (bf16[64,256]{1,0:T(8,128)(2,1)}, bf16[64,256]{1,0:T(8,128)(2,1)S(1)}, u32[]{:S(2)}, u32[]{:S(2)}) collective-permute-start(bf16[64,256]{1,0:T(8,128)(2,1)} %get-tuple-element.27), channel_id=1, source_target_pairs={{0,0},{1,128},{64,1},{65,129},{128,64},{129,192},{192,65},{193,193... | collective-permute-start | bytes 98312 | tf_op jit(solution)/shard_map/ppermute | solution.py:263
  15.2 9.2 %collective-permute-start.5 = (bf16[64,256]{1,0:T(8,128)(2,1)}, bf16[64,256]{1,0:T(8,128)(2,1)S(1)}, u32[]{:S(2)}, u32[]{:S(2)}) collective-permute-start(bf16[64,256]{1,0:T(8,128)(2,1)} %get-tuple-element.28), channel_id=1, source_target_pairs={{0,1},{1,129},{64,0},{65,128},{128,65},{129,193},{192,64},{193,192... | collective-permute-start | bytes 98312 | tf_op jit(solution)/shard_map/ppermute | solution.py:263
  16.2 10.0 %collective-permute-start.6 = (bf16[64,256]{1,0:T(8,128)(2,1)}, bf16[64,256]{1,0:T(8,128)(2,1)S(1)}, u32[]{:S(2)}, u32[]{:S(2)}) collective-permute-start(bf16[64,256]{1,0:T(8,128)(2,1)} %get-tuple-element.29), channel_id=1, source_target_pairs={{0,64},{1,192},{64,65},{65,193},{128,0},{129,128},{192,1},{193,129... | collective-permute-start | bytes 98312 | tf_op jit(solution)/shard_map/ppermute | solution.py:263
  16.5 9.8 %collective-permute-start.7 = (bf16[64,256]{1,0:T(8,128)(2,1)}, bf16[64,256]{1,0:T(8,128)(2,1)S(1)}, u32[]{:S(2)}, u32[]{:S(2)}) collective-permute-start(bf16[64,256]{1,0:T(8,128)(2,1)} %get-tuple-element.30), channel_id=1, source_target_pairs={{0,65},{1,193},{64,64},{65,192},{128,1},{129,129},{192,0},{193,128... | collective-permute-start | bytes 98312 | tf_op jit(solution)/shard_map/ppermute | solution.py:263
  18.5 0.6 copy-start.12
  20.6 5.7 %collective-permute-start.9 = (bf16[32,256]{1,0:T(8,128)(2,1)}, bf16[32,256]{1,0:T(8,128)(2,1)S(1)}, u32[]{:S(2)}, u32[]{:S(2)}) collective-permute-start(bf16[32,256]{1,0:T(8,128)(2,1)} %get-tuple-element.34), channel_id=1, source_target_pairs={{0,64},{64,128},{128,192},{192,0},{1,65},{65,129},{129,193},{193,1... | collective-permute-start | bytes 49160 | tf_op jit(solution)/shard_map/ppermute | solution.py:256
  23.7 4.3 %copy-start.8 = (bf16[64,256]{1,0:T(8,128)(2,1)}, bf16[64,256]{1,0:T(8,128)(2,1)S(1)}, u32[]{:S(2)}) copy-start(bf16[64,256]{1,0:T(8,128)(2,1)S(1)} %collective-permute-done.4.refs_0_) | copy-start | bytes 98308
  23.7 4.3 %collective-permute-start.10 = (bf16[32,256]{1,0:T(8,128)(2,1)}, bf16[32,256]{1,0:T(8,128)(2,1)S(1)}, u32[]{:S(2)}, u32[]{:S(2)}) collective-permute-start(bf16[32,256]{1,0:T(8,128)(2,1)} %get-tuple-element.35), channel_id=1, source_target_pairs={{0,128},{64,192},{128,0},{192,64},{1,129},{65,193},{129,1},{193,65... | collective-permute-start | bytes 49160 | tf_op jit(solution)/shard_map/ppermute | solution.py:256
  24.4 3.7 %copy-start.9 = (bf16[64,256]{1,0:T(8,128)(2,1)}, bf16[64,256]{1,0:T(8,128)(2,1)S(1)}, u32[]{:S(2)}) copy-start(bf16[64,256]{1,0:T(8,128)(2,1)S(1)} %collective-permute-done.5.refs_1_) | copy-start | bytes 98308
  24.4 3.6 %collective-permute-start.11 = (bf16[32,256]{1,0:T(8,128)(2,1)}, bf16[32,256]{1,0:T(8,128)(2,1)S(1)}, u32[]{:S(2)}, u32[]{:S(2)}) collective-permute-start(bf16[32,256]{1,0:T(8,128)(2,1)} %get-tuple-element.36), channel_id=1, source_target_pairs={{0,192},{64,0},{128,64},{192,128},{1,193},{65,1},{129,65},{193,129... | collective-permute-start | bytes 49160 | tf_op jit(solution)/shard_map/ppermute | solution.py:256
  26.2 1.8 %copy-start.10 = (bf16[64,256]{1,0:T(8,128)(2,1)}, bf16[64,256]{1,0:T(8,128)(2,1)S(1)}, u32[]{:S(2)}) copy-start(bf16[64,256]{1,0:T(8,128)(2,1)S(1)} %collective-permute-done.6.refs_2_) | copy-start | bytes 98308
  26.2 1.8 %copy-start.11 = (bf16[64,256]{1,0:T(8,128)(2,1)}, bf16[64,256]{1,0:T(8,128)(2,1)S(1)}, u32[]{:S(2)}) copy-start(bf16[64,256]{1,0:T(8,128)(2,1)S(1)} %collective-permute-done.7.refs_3_) | copy-start | bytes 98308
  26.3 1.8 %copy-start.13 = (bf16[32,256]{1,0:T(8,128)(2,1)}, bf16[32,256]{1,0:T(8,128)(2,1)S(1)}, u32[]{:S(2)}) copy-start(bf16[32,256]{1,0:T(8,128)(2,1)S(1)} %collective-permute-done.9.refs_5_) | copy-start | bytes 49156
  28.0 0.6 copy-start.14
  28.0 0.6 copy-start.15
  30.2 5.7 %collective-permute-start.14 = (bf16[4,96,256]{2,1,0:T(8,128)(2,1)}, bf16[4,96,256]{2,1,0:T(8,128)(2,1)S(1)}, u32[]{:S(2)}, u32[]{:S(2)}) collective-permute-start(bf16[4,96,256]{2,1,0:T(8,128)(2,1)} %join.1), channel_id=1, source_target_pairs={{0,48},{16,0},{32,16},{48,32},{1,49},{17,1},{33,17},{49,33},{2,50}... | collective-permute-start | bytes 589832 | tf_op jit(solution)/shard_map/ppermute | solution.py:256
  31.8 17.1 %collective-permute-start.13 = (bf16[4,96,256]{2,1,0:T(8,128)(2,1)}, bf16[4,96,256]{2,1,0:T(8,128)(2,1)S(1)}, u32[]{:S(2)}, u32[]{:S(2)}) collective-permute-start(bf16[4,96,256]{2,1,0:T(8,128)(2,1)} %join.1), channel_id=1, source_target_pairs={{0,32},{16,48},{32,0},{48,16},{1,33},{17,49},{33,1},{49,17},{2,34}... | collective-permute-start | bytes 589832 | tf_op jit(solution)/shard_map/ppermute | solution.py:256
  32.1 16.9 %collective-permute-start.12 = (bf16[4,96,256]{2,1,0:T(8,128)(2,1)}, bf16[4,96,256]{2,1,0:T(8,128)(2,1)S(1)}, u32[]{:S(2)}, u32[]{:S(2)}) collective-permute-start(bf16[4,96,256]{2,1,0:T(8,128)(2,1)} %join.1), channel_id=1, source_target_pairs={{0,16},{16,32},{32,48},{48,0},{1,17},{17,33},{33,49},{49,1},{2,18}... | collective-permute-start | bytes 589832 | tf_op jit(solution)/shard_map/ppermute | solution.py:256
  49.0 3.9 %copy-start.19 = (bf16[64,768]{1,0:T(8,128)(2,1)S(1)}, bf16[64,768]{1,0:T(8,128)(2,1)}, u32[]{:S(2)}) copy-start(bf16[64,768]{1,0:T(8,128)(2,1)} %get-tuple-element.23) | copy-start | bytes 294916
  49.0 9.6 %copy-start.18 = (bf16[64,768]{1,0:T(8,128)(2,1)S(1)}, bf16[64,768]{1,0:T(8,128)(2,1)}, u32[]{:S(2)}) copy-start(bf16[64,768]{1,0:T(8,128)(2,1)} %get-tuple-element.24) | copy-start | bytes 294916
  49.0 11.3 %copy-start.17 = (bf16[64,768]{1,0:T(8,128)(2,1)S(1)}, bf16[64,768]{1,0:T(8,128)(2,1)}, u32[]{:S(2)}) copy-start(bf16[64,768]{1,0:T(8,128)(2,1)} %get-tuple-element.25) | copy-start | bytes 294916
  49.0 18.9 %copy-start.16 = (bf16[64,768]{1,0:T(8,128)(2,1)S(1)}, bf16[64,768]{1,0:T(8,128)(2,1)}, u32[]{:S(2)}) copy-start(bf16[64,768]{1,0:T(8,128)(2,1)} %get-tuple-element.26) | copy-start | bytes 294916
  50.1 17.8 %collective-permute-start.16 = (bf16[4,4,96,256]{3,2,1,0:T(8,128)(2,1)S(1)}, bf16[4,4,96,256]{3,2,1,0:T(8,128)(2,1)S(1)}, u32[]{:S(2)}, u32[]{:S(2)}) collective-permute-start(bf16[4,4,96,256]{3,2,1,0:T(8,128)(2,1)S(1)} %pad_maximum_fusion.refs_4_), channel_id=1, source_target_pairs={{0,12},{4,0},{8,4},{12,8},{1,13},{5,1},{9,5},{13,9},{2,14},{6,2},{... | collective-permute-start | bytes 2359304 | tf_op jit(solution)/shard_map/ppermute | solution.py:256
  52.9 18.3 %collective-permute-start.15 = (bf16[4,4,96,256]{3,2,1,0:T(8,128)(2,1)S(1)}, bf16[4,4,96,256]{3,2,1,0:T(8,128)(2,1)S(1)}, u32[]{:S(2)}, u32[]{:S(2)}) collective-permute-start(bf16[4,4,96,256]{3,2,1,0:T(8,128)(2,1)S(1)} %pad_maximum_fusion.refs_4_), channel_id=1, source_target_pairs={{0,4},{4,8},{8,12},{12,0},{1,5},{5,9},{9,13},{13,1},{2,6},{6,10},{... | collective-permute-start | bytes 2359304 | tf_op jit(solution)/shard_map/ppermute | solution.py:256
  52.9 21.2 %collective-permute-start = (bf16[64,768]{1,0:T(8,128)(2,1)S(1)}, bf16[64,768]{1,0:T(8,128)(2,1)S(1)}, u32[]{:S(2)}, u32[]{:S(2)}) collective-permute-start(bf16[64,768]{1,0:T(8,128)(2,1)S(1)} %copy-done.19), channel_id=1, source_target_pairs={{0,0},{1,128},{64,1},{65,129},{128,64},{129,192},{192,65},{193,193... | collective-permute-start | bytes 294920 | tf_op jit(solution)/shard_map/ppermute | solution.py:264
  58.6 17.7 %collective-permute-start.1 = (bf16[64,768]{1,0:T(8,128)(2,1)S(1)}, bf16[64,768]{1,0:T(8,128)(2,1)S(1)}, u32[]{:S(2)}, u32[]{:S(2)}) collective-permute-start(bf16[64,768]{1,0:T(8,128)(2,1)S(1)} %copy-done.18), channel_id=1, source_target_pairs={{0,1},{1,129},{64,0},{65,128},{128,65},{129,193},{192,64},{193,192... | collective-permute-start | bytes 294920 | tf_op jit(solution)/shard_map/ppermute | solution.py:264
  60.3 16.0 %collective-permute-start.2 = (bf16[64,768]{1,0:T(8,128)(2,1)S(1)}, bf16[64,768]{1,0:T(8,128)(2,1)S(1)}, u32[]{:S(2)}, u32[]{:S(2)}) collective-permute-start(bf16[64,768]{1,0:T(8,128)(2,1)S(1)} %copy-done.17), channel_id=1, source_target_pairs={{0,64},{1,192},{64,65},{65,193},{128,0},{129,128},{192,1},{193,129... | collective-permute-start | bytes 294920 | tf_op jit(solution)/shard_map/ppermute | solution.py:264
  67.9 9.2 %collective-permute-start.3 = (bf16[64,768]{1,0:T(8,128)(2,1)S(1)}, bf16[64,768]{1,0:T(8,128)(2,1)S(1)}, u32[]{:S(2)}, u32[]{:S(2)}) collective-permute-start(bf16[64,768]{1,0:T(8,128)(2,1)S(1)} %copy-done.16), channel_id=1, source_target_pairs={{0,65},{1,193},{64,64},{65,192},{128,1},{129,129},{192,0},{193,128... | collective-permute-start | bytes 294920 | tf_op jit(solution)/shard_map/ppermute | solution.py:264
  71.1 20.1 %copy-start = (s32[64]{0:T(128)S(1)}, s32[64]{0:T(128)}, u32[]{:S(2)}) copy-start(s32[64]{0:T(128)} %owner_ref.1) | copy-start | bytes 772
  71.2 20.1 %copy-start.1 = (s32[4]{0:T(128)S(1)}, s32[4]{0:T(128)}, u32[]{:S(2)}) copy-start(s32[4]{0:T(128)} %window_ref.1) | copy-start | bytes 52
  71.2 17.8 %collective-permute-start.19 = (bf16[4,4,96,256]{3,2,1,0:T(8,128)(2,1)S(1)}, bf16[4,4,96,256]{3,2,1,0:T(8,128)(2,1)S(1)}, u32[]{:S(2)}, u32[]{:S(2)}) collective-permute-start(bf16[4,4,96,256]{3,2,1,0:T(8,128)(2,1)S(1)} %pad_maximum_fusion.refs_4_), channel_id=1, source_target_pairs={{0,1},{1,0},{2,3},{3,2},{4,5},{5,4},{6,7},{7,6},{8,9},{9,8},{10,11... | collective-permute-start | bytes 2359304 | tf_op jit(solution)/shard_map/ppermute | solution.py:256
  74.1 10.8 %collective-permute-start.18 = (bf16[2,4,96,256]{3,2,1,0:T(8,128)(2,1)S(1)}, bf16[2,4,96,256]{3,2,1,0:T(8,128)(2,1)S(1)}, u32[]{:S(2)}, u32[]{:S(2)}) collective-permute-start(bf16[2,4,96,256]{3,2,1,0:T(8,128)(2,1)S(1)} %slice.9), channel_id=1, source_target_pairs={{0,12},{4,0},{8,4},{12,8},{1,13},{5,1},{9,5},{13,9},{2,14},{6,2},{... | collective-permute-start | bytes 1179656 | tf_op jit(solution)/shard_map/ppermute | solution.py:256
  76.3 11.6 %collective-permute-start.17 = (bf16[2,4,96,256]{3,2,1,0:T(8,128)(2,1)S(1)}, bf16[2,4,96,256]{3,2,1,0:T(8,128)(2,1)S(1)}, u32[]{:S(2)}, u32[]{:S(2)}) collective-permute-start(bf16[2,4,96,256]{3,2,1,0:T(8,128)(2,1)S(1)} %slice.8), channel_id=1, source_target_pairs={{0,4},{4,8},{8,12},{12,0},{1,5},{5,9},{9,13},{13,1},{2,6},{6,10},{... | collective-permute-start | bytes 1179656 | tf_op jit(solution)/shard_map/ppermute | solution.py:256
  76.3 12.7 %collective-permute-start.21 = (bf16[4,4,96,256]{3,2,1,0:T(8,128)(2,1)S(1)}, bf16[4,4,96,256]{3,2,1,0:T(8,128)(2,1)S(1)}, u32[]{:S(2)}, u32[]{:S(2)}) collective-permute-start(bf16[4,4,96,256]{3,2,1,0:T(8,128)(2,1)S(1)} %collective-permute-done.16.refs_6_), channel_id=1, source_target_pairs={{0,1},{1,0},{2,3},{3,2},{4,5},{5,4},{6,7},{7,6},{8,9},{9,8},{10,11... | collective-permute-start | bytes 2359304 | tf_op jit(solution)/shard_map/ppermute | solution.py:256
  77.1 13.3 %collective-permute-start.20 = (bf16[4,4,96,256]{3,2,1,0:T(8,128)(2,1)S(1)}, bf16[4,4,96,256]{3,2,1,0:T(8,128)(2,1)S(1)}, u32[]{:S(2)}, u32[]{:S(2)}) collective-permute-start(bf16[4,4,96,256]{3,2,1,0:T(8,128)(2,1)S(1)} %collective-permute-done.15.refs_5_), channel_id=1, source_target_pairs={{0,1},{1,0},{2,3},{3,2},{4,5},{5,4},{6,7},{7,6},{8,9},{9,8},{10,11... | collective-permute-start | bytes 2359304 | tf_op jit(solution)/shard_map/ppermute | solution.py:256
  84.9 4.1 %collective-permute-start.23 = (bf16[2,4,96,256]{3,2,1,0:T(8,128)(2,1)S(1)}, bf16[2,4,96,256]{3,2,1,0:T(8,128)(2,1)S(1)}, u32[]{:S(2)}, u32[]{:S(2)}) collective-permute-start(bf16[2,4,96,256]{3,2,1,0:T(8,128)(2,1)S(1)} %collective-permute-done.18.refs_8_), channel_id=1, source_target_pairs={{0,1},{1,0},{2,3},{3,2},{4,5},{5,4},{6,7},{7,6},{8,9},{9,8},{10,11... | collective-permute-start | bytes 1179656 | tf_op jit(solution)/shard_map/ppermute | solution.py:256
  87.9 2.5 %collective-permute-start.22 = (bf16[2,4,96,256]{3,2,1,0:T(8,128)(2,1)S(1)}, bf16[2,4,96,256]{3,2,1,0:T(8,128)(2,1)S(1)}, u32[]{:S(2)}, u32[]{:S(2)}) collective-permute-start(bf16[2,4,96,256]{3,2,1,0:T(8,128)(2,1)S(1)} %collective-permute-done.17.refs_7_), channel_id=1, source_target_pairs={{0,1},{1,0},{2,3},{3,2},{4,5},{5,4},{6,7},{7,6},{8,9},{9,8},{10,11... | collective-permute-start | bytes 1179656 | tf_op jit(solution)/shard_map/ppermute | solution.py:256
  89.0 1.3 copy-start.2
  90.4 0.9 copy-start.3
  147.2 9.8 %collective-permute-start.24 = (bf16[64,768]{1,0:T(8,128)(2,1)S(1)}, bf16[64,768]{1,0:T(8,128)(2,1)S(1)}, u32[]{:S(2)}, u32[]{:S(2)}) collective-permute-start(bf16[64,768]{1,0:T(8,128)(2,1)S(1)} %get-tuple-element.37), channel_id=1, source_target_pairs={{0,0},{128,1},{1,64},{129,65},{64,128},{192,129},{65,192},{193,193... | collective-permute-start | bytes 294920 | tf_op jit(solution)/shard_map/ppermute | solution.py:277
  151.6 5.4 %collective-permute-start.25 = (bf16[64,768]{1,0:T(8,128)(2,1)S(1)}, bf16[64,768]{1,0:T(8,128)(2,1)S(1)}, u32[]{:S(2)}, u32[]{:S(2)}) collective-permute-start(bf16[64,768]{1,0:T(8,128)(2,1)S(1)} %get-tuple-element.38), channel_id=1, source_target_pairs={{1,0},{129,1},{0,64},{128,65},{65,128},{193,129},{64,192},{192,193... | collective-permute-start | bytes 294920 | tf_op jit(solution)/shard_map/ppermute | solution.py:277
  151.7 6.0 %collective-permute-start.26 = (bf16[64,768]{1,0:T(8,128)(2,1)S(1)}, bf16[64,768]{1,0:T(8,128)(2,1)S(1)}, u32[]{:S(2)}, u32[]{:S(2)}) collective-permute-start(bf16[64,768]{1,0:T(8,128)(2,1)S(1)} %get-tuple-element.39), channel_id=1, source_target_pairs={{64,0},{192,1},{65,64},{193,65},{0,128},{128,129},{1,192},{129,193... | collective-permute-start | bytes 294920 | tf_op jit(solution)/shard_map/ppermute | solution.py:277
  152.5 6.9 %collective-permute-start.27 = (bf16[64,768]{1,0:T(8,128)(2,1)S(1)}, bf16[64,768]{1,0:T(8,128)(2,1)S(1)}, u32[]{:S(2)}, u32[]{:S(2)}) collective-permute-start(bf16[64,768]{1,0:T(8,128)(2,1)S(1)} %get-tuple-element.40), channel_id=1, source_target_pairs={{65,0},{193,1},{64,64},{192,65},{1,128},{129,129},{0,192},{128,193... | collective-permute-start | bytes 294920 | tf_op jit(solution)/shard_map/ppermute | solution.py:277
  157.0 2.4 %copy-start.4 = (bf16[64,768]{1,0:T(8,128)(2,1)}, bf16[64,768]{1,0:T(8,128)(2,1)S(1)}, u32[]{:S(2)}) copy-start(bf16[64,768]{1,0:T(8,128)(2,1)S(1)} %collective-permute-done.24.refs_0_) | copy-start | bytes 294916
  157.0 2.4 %copy-start.5 = (bf16[64,768]{1,0:T(8,128)(2,1)}, bf16[64,768]{1,0:T(8,128)(2,1)S(1)}, u32[]{:S(2)}) copy-start(bf16[64,768]{1,0:T(8,128)(2,1)S(1)} %collective-permute-done.25.refs_1_) | copy-start | bytes 294916
  157.7 1.7 %copy-start.6 = (bf16[64,768]{1,0:T(8,128)(2,1)}, bf16[64,768]{1,0:T(8,128)(2,1)S(1)}, u32[]{:S(2)}) copy-start(bf16[64,768]{1,0:T(8,128)(2,1)S(1)} %collective-permute-done.26.refs_2_) | copy-start | bytes 294916
  159.4 0.6 copy-start.7
